TPU v7x, 1024 devices: a whole 4x8x16 slice. The times are simulated.
1024 devices in a mesh: section: 4 (over y_hi), ctx: 32 (over z, y_lo), tp: 8 (over x, core).
Axes of the slice: x: 4, y: 8 (y_hi: 4, y_lo: 2; y = y_hi * 2 + y_lo), z: 16, core: 2. Of those that a mesh axis runs over, the one named last changes fastest.
Arguments:
- mamba_input: bfloat16 [4, 4096, 8192], P('section', 'ctx', 'tp'), may hold values from -6 to 6
- mamba_gate: bfloat16 [4, 4096, 8192], P('section', 'ctx', 'tp'), may hold values from -6 to 6
- write_vectors: bfloat16 [4, 4096, 1024], P('section', 'ctx', 'tp'), may hold values from -0.546875 to 0.546875
- read_vectors: bfloat16 [4, 4096, 1024], P('section', 'ctx', 'tp'), may hold values from -6 to 6
- step_sizes: float32 [4, 128, 4096], P('section', 'tp', 'ctx'), may hold values from 0.05 to 0.5
- decay_rates: float32 [4, 128], P('section', 'tp'), may hold values from 0.0002 to 0.3
- skip_scale: float32 [4, 128], P('section', 'tp'), may hold values from 0.5 to 1.5
- norm_gain: float32 [4, 8192], P('section', 'tp'), may hold values from 0.5 to 1.5
- attn_queries: bfloat16 [4, 4096, 4096], P('section', 'ctx', 'tp'), may hold values from -180 to 180
- attn_keys: bfloat16 [4, 4096, 1024], P('section', 'ctx', 'tp'), may hold values from -8 to 8
- attn_values: bfloat16 [4, 4096, 1024], P('section', 'ctx', 'tp'), may hold values from -6 to 6
- block_order: int32 [4, 64], P('section'), may hold values from 0 to 63, each once within a row
Outputs:
- handed: bfloat16 [4, 4096, 8192], P('section', 'ctx', 'tp')
- attended: bfloat16 [4, 4096, 4096], P('section', 'ctx', 'tp')
Inputs may be any that keep to these rules, and one draw needn't show every extreme that they name: Each row of block_order names every half-block 0 to 63 once.
All inputs are finite; a program needn't handle non-finite values.
Results may differ from a plain program's by a relative error of at most 0.0095.
Values may be sent and summed in bfloat16 or wider, within the bound.
A program may use at most 64 MiB of HBM per device.

v0:
```python
import jax
import jax.numpy as jnp
from jax import lax
from jax.sharding import PartitionSpec as P

SPAN = 128
MHEADS = 128
HEADP = 64
NSTATE = 128
GROUPS = 8
AHEADS = 32
KVHEADS = 8
HEADD = 128


def in_blocks(array, dim, devices):
    lengths = array.shape
    tiles = array.reshape(*lengths[:dim], devices, lengths[dim] // devices, *lengths[dim + 1 :])
    return jnp.moveaxis(tiles, dim, 0)


def piece_ends(length, count):
    hop = length // count
    if hop >= 8:
        hop -= hop % 8
    return [hop * k for k in range(1, count)]


def joined_along(tiles, dim):
    tiles = jnp.moveaxis(tiles, 0, dim)
    lengths = tiles.shape
    return tiles.reshape(*lengths[:dim], lengths[dim] * lengths[dim + 1], *lengths[dim + 2 :])


def exchange_in_pieces(array, axis, pieces, split_dim, concat_dim):
    tiles = in_blocks(array, split_dim, lax.axis_size(axis))
    split_at = max(range(1, max(2, tiles.ndim - 1)), key=lambda d: tiles.shape[d])
    gathered = []
    for share in jnp.split(tiles, piece_ends(tiles.shape[split_at], pieces), axis=split_at):
        if share.size:
            gathered.append(lax.all_to_all(share, axis, split_axis=0, concat_axis=0, tiled=True))
    return joined_along(jnp.concatenate(gathered, axis=split_at), concat_dim)


def from_everyone(array, axis):
    devices = lax.axis_size(axis)
    return lax.all_to_all(
        jnp.broadcast_to(array[None], (devices, *array.shape)), axis, 0, 0, tiled=True
    )


def gathered_copies(array, axis, dim):
    return joined_along(from_everyone(array, axis), dim)


def passed_along(block, axis, distance):
    devices = range(lax.axis_size(axis))
    route = [((i - distance) % len(devices), i) for i in devices]
    return lax.ppermute(block, axis, route)


def sent_together(arrays, axis, dim, along):
    widths = [a.shape[along] for a in arrays]
    both = jnp.concatenate(arrays, axis=along)
    filled = lax.all_gather(both, axis, axis=dim, tiled=True)
    return tuple(jnp.split(filled, [sum(widths[:k]) for k in range(1, len(widths))], axis=along))


def positions_of(order, first_row, count, half_len):
    row_index = first_row + jnp.arange(count, dtype=jnp.int32)
    block_index = row_index // half_len
    table_index = jnp.arange(order.shape[0], dtype=jnp.int32)
    offsets = jnp.sum(
        jnp.where(block_index[:, None] == table_index[None, :], order[None, :], 0), axis=1
    )
    return offsets * half_len + row_index % half_len


def prefix_step(carry, item):
    decay_row, piece = item
    return (decay_row[:, None] * carry + piece, carry)


def shards(
    mamba_input,
    mamba_gate,
    write_vectors,
    read_vectors,
    step_sizes,
    decay_rates,
    skip_scale,
    norm_gain,
    attn_queries,
    attn_keys,
    attn_values,
    block_order,
):
    tok_rows = mamba_input.shape[1]
    heads_here = decay_rates.shape[1]
    groups_here = write_vectors.shape[2] // NSTATE
    per_group = MHEADS // GROUPS
    span_count = tok_rows // SPAN
    x_spans = mamba_input[0].reshape(span_count, SPAN, heads_here, HEADP)
    write_spans = write_vectors[0].reshape(span_count, SPAN, groups_here, NSTATE)
    read_spans = read_vectors[0].reshape(span_count, SPAN, groups_here, NSTATE)
    step_spans = step_sizes[0].reshape(heads_here, span_count, SPAN)
    rates = decay_rates[0]
    skips = skip_scale[0]
    lower = jnp.tril(jnp.ones((SPAN, SPAN), dtype=bool))
    span_idx = 0
    x_span = x_spans[span_idx]
    write_span = write_spans[span_idx]
    read_span = read_spans[span_idx]
    step_span = step_spans[:, span_idx]
    log_decay = jnp.cumsum(-rates[:, None] * step_span, axis=1)
    intersections = jnp.einsum(
        "tgn,sgn->gts", read_span, write_span, preferred_element_type=jnp.float32
    )
    intersections = jnp.repeat(intersections, per_group, axis=0)
    spread = log_decay[:, :, None] - log_decay[:, None, :]
    decay_pairs = jnp.exp(jnp.where(lower[None], spread, 0.0))
    mixing = jnp.where(
        lower[None], intersections * decay_pairs * step_span[:, None, :], 0.0
    ).astype(jnp.bfloat16)
    inner = jnp.einsum("hts,shp->thp", mixing, x_span, preferred_element_type=jnp.float32)
    to_end = step_span * jnp.exp(log_decay[:, -1:] - log_decay)
    weighted = (x_span.astype(jnp.float32) * to_end.T[:, :, None]).astype(jnp.bfloat16)
    contrib = jnp.einsum(
        "sgkp,sgn->gkpn",
        weighted.reshape(SPAN, groups_here, per_group, HEADP),
        write_span,
        preferred_element_type=jnp.float32,
    )
    inner_list = [inner]
    log_list = [log_decay]
    contrib_list = [contrib.reshape(heads_here, HEADP, NSTATE)]
    running = jnp.zeros((heads_here, HEADP, NSTATE), jnp.float32)
    total = jnp.ones((heads_here,), jnp.float32)
    before_list = []
    span_idx = 0
    before_list.append(running)
    decay_before = [total]
    span_decay = jnp.exp(log_list[span_idx][:, -1])
    running = span_decay[:, None, None] * running + contrib_list[span_idx]
    total = total * span_decay
    flat_state = running.reshape(1, heads_here, HEADP * NSTATE)
    slices_in = exchange_in_pieces(flat_state.astype(jnp.bfloat16), "ctx", 2, 2, 0).astype(
        flat_state.dtype
    )
    all_totals = gathered_copies(total[None], "ctx", 0)
    prefixed = lax.scan(prefix_step, jnp.zeros_like(slices_in[0]), (all_totals, slices_in))[1]
    incoming = (
        lax.all_to_all(
            prefixed.astype(jnp.bfloat16), "ctx", split_axis=0, concat_axis=2, tiled=True
        )
        .astype(prefixed.dtype)
        .reshape(heads_here, HEADP, NSTATE)
    )
    span_idx = 0
    entering = decay_before[span_idx][:, None, None] * incoming
    read_float = read_spans[span_idx].astype(jnp.float32)
    carried = jnp.einsum(
        "tgn,gkpn->tgkp",
        read_float,
        entering.reshape(groups_here, per_group, HEADP, NSTATE),
        precision=lax.Precision.HIGHEST,
    )
    carried = carried.reshape(SPAN, heads_here, HEADP) * jnp.exp(log_list[span_idx]).T[:, :, None]
    output_list = (
        inner_list[span_idx]
        + carried
        + skips[None, :, None] * x_spans[span_idx].astype(jnp.float32)
    )
    gated = output_list * jax.nn.silu(
        mamba_gate[0].reshape(tok_rows, heads_here, HEADP).astype(jnp.float32)
    )
    grouped = gated.reshape(tok_rows, groups_here, per_group * HEADP)
    factor = lax.rsqrt(jnp.mean(grouped * grouped, axis=-1, keepdims=True) + 1e-05)
    normed = grouped * factor * norm_gain[0].reshape(groups_here, per_group * HEADP)[None]
    mixed = normed.astype(jnp.bfloat16).reshape(1, tok_rows, heads_here * HEADP)
    handed = passed_along(mixed, "section", 1)
    per_kv = AHEADS // KVHEADS
    kv_here = attn_keys.shape[2] // HEADD
    half_len = tok_rows // 2
    order = block_order[0]
    query_rows = attn_queries[0].reshape(tok_rows, kv_here, per_kv, HEADD)
    query_pos = positions_of(order, lax.axis_index("ctx") * tok_rows, tok_rows, half_len)
    scale = 1.0 / jnp.sqrt(jnp.float32(HEADD))
    key_piece, value_piece = sent_together((attn_keys[0], attn_values[0]), "ctx", 0, 1)
    count = key_piece.shape[0]
    key_heads = key_piece.reshape(count, kv_here, HEADD)
    value_heads = value_piece.reshape(count, kv_here, HEADD)
    key_pos = positions_of(order, jnp.int32(0), count, half_len)
    peak = jnp.full((kv_here, per_kv, tok_rows), -1e30, jnp.float32)
    visible = key_pos[None, None, None, :] <= query_pos[None, None, :, None]
    scores = (
        jnp.einsum("tgqd,kgd->gqtk", query_rows, key_heads, preferred_element_type=jnp.float32)
        * scale
    )
    masked = jnp.where(visible, scores, -1e30)
    new_peak = jnp.maximum(peak, jnp.max(masked, axis=3))
    weights = jnp.where(visible, jnp.exp(masked - new_peak[..., None]), 0.0)
    total_w = jnp.sum(weights, axis=3)
    accum = jnp.einsum(
        "gqtk,kgd->gqtd",
        weights.astype(jnp.bfloat16),
        value_heads,
        preferred_element_type=jnp.float32,
    )
    peak, total_w, accum = (new_peak, total_w, accum)
    result = accum / total_w[..., None]
    attended = (
        result.transpose(2, 0, 1, 3)
        .reshape(1, tok_rows, kv_here * per_kv * HEADD)
        .astype(jnp.bfloat16)
    )
    return (handed, attended)


def solution(mesh):
    return jax.shard_map(
        shards,
        mesh=mesh,
        in_specs=(
            P("section", "ctx", "tp"),
            P("section", "ctx", "tp"),
            P("section", "ctx", "tp"),
            P("section", "ctx", "tp"),
            P("section", "tp", "ctx"),
            P("section", "tp"),
            P("section", "tp"),
            P("section", "tp"),
            P("section", "ctx", "tp"),
            P("section", "ctx", "tp"),
            P("section", "ctx", "tp"),
            P("section", None),
        ),
        out_specs=(P("section", "ctx", "tp"), P("section", "ctx", "tp")),
        check_vma=False,
    )
```

profile of v0, /device:TPU:6, one launch (start us, length us, event | category | flops | bytes accessed | tf_op | source)
XLA Modules:
  0.0 215.2 jit_solution(14667686828382856147)
XLA Ops:
  7.2 0.7 negate_bitcast_fusion
  7.9 0.8 broadcast_multiply_fusion
  9.1 0.8 exponential_bitcast_fusion
  9.9 1.1 copy.45
  11.8 0.7 fusion.49
  12.5 36.3 %all_to_all.30 = bf16[32,1,8,256]{3,2,1,0:T(8,128)(2,1)S(1)} all-to-all(bf16[32,1,8,256]{3,2,1,0:T(8,128)(2,1)S(1)} %get-tuple-element.66), channel_id=1, replica_groups=mesh['section'=4,'ctx'=32,'tp'=8] {'ctx'}, dimensions={0} | all-to-all | bytes 262144 | tf_op jit(solution)/shard_map/all_to_all | solution.py:41
  48.8 3.9 %all-to-all-start.2 = ((bf16[32,1,8,256]{3,2,1,0:T(8,128)(2,1)}), bf16[32,1,8,256]{3,2,1,0:T(8,128)(2,1)S(1)}, u32[]{:S(2)}, u32[]{:S(2)}) async-start(bf16[32,1,8,256]{3,2,1,0:T(8,128)(2,1)} %get-tuple-element.67), calls=%async_computation.2 | async-start | bytes 262144 | tf_op jit(solution)/shard_map/all_to_all | solution.py:41
  52.7 1.4 pad_maximum_fusion
  54.1 1.1 copy.49
  55.3 12.6 %all-to-all-done.2 = bf16[32,1,8,256]{3,2,1,0:T(8,128)(2,1)S(1)} async-done(((bf16[32,1,8,256]{3,2,1,0:T(8,128)(2,1)}), bf16[32,1,8,256]{3,2,1,0:T(8,128)(2,1)S(1)}, u32[]{:S(2)}, u32[]{:S(2)}) %all-to-all-start.2) | async-done | bytes 131104 | tf_op jit(solution)/shard_map/all_to_all | solution.py:41
  67.9 0.6 broadcast_in_dim.108
  68.5 3.8 %all-to-all-start = ((f32[32,1,16]{2,1,0:T(1,128)}), f32[32,1,16]{2,1,0:T(1,128)S(1)}, u32[]{:S(2)}, u32[]{:S(2)}) async-start(f32[32,1,16]{2,1,0:T(1,128)} %broadcast_in_dim.108), calls=%async_computation | async-start | bytes 32768 | tf_op jit(solution)/shard_map/all_to_all | solution.py:47
  72.4 13.1 %all-to-all-done = f32[32,1,16]{2,1,0:T(1,128)S(1)} async-done(((f32[32,1,16]{2,1,0:T(1,128)}), f32[32,1,16]{2,1,0:T(1,128)S(1)}, u32[]{:S(2)}, u32[]{:S(2)}) %all-to-all-start) | async-done | bytes 2080 | tf_op jit(solution)/shard_map/all_to_all | solution.py:47
  85.5 21.8 %while.13 = (s32[]{:T(128)}, f32[16,256]{1,0:T(8,128)S(1)}, bf16[32,16,256]{2,1,0:T(8,128)(2,1)}, f32[32,16]{1,0:T(8,128)S(1)}, f32[32,16,256]{2,1,0:T(8,128)S(1)}, /*index=5*/s32[]{:T(128)}, s32[]{:T(128)}) while((s32[]{:T(128)}, f32[16,256]{1,0:T(8,128)S(1)}, bf16[32,16,256]{2,1,0:T(8,128)(2,1)}, f32[32,16]{1,0:T(8,128)S(1)}, ...), condition=%wide.region_2.3_spmd.clone, body=%wide.region_1.2_spmd.clone.sunk | while | flops 16387 | bytes 74028 | solution.py:151
  85.5 0.6 bitcast_dynamic-update-slice_fusion.2
  86.2 0.6 bitcast_dynamic-update-slice_fusion.2
  86.9 0.6 bitcast_dynamic-update-slice_fusion.2
  87.6 0.6 bitcast_dynamic-update-slice_fusion.2
  88.3 0.6 bitcast_dynamic-update-slice_fusion.2
  88.9 0.6 bitcast_dynamic-update-slice_fusion.2
  89.6 0.6 bitcast_dynamic-update-slice_fusion.2
  90.3 0.6 bitcast_dynamic-update-slice_fusion.2
  91.0 0.6 bitcast_dynamic-update-slice_fusion.2
  91.7 0.6 bitcast_dynamic-update-slice_fusion.2
  92.3 0.6 bitcast_dynamic-update-slice_fusion.2
  93.0 0.6 bitcast_dynamic-update-slice_fusion.2
  93.7 0.6 bitcast_dynamic-update-slice_fusion.2
  94.4 0.6 bitcast_dynamic-update-slice_fusion.2
  95.1 0.6 bitcast_dynamic-update-slice_fusion.2
  96.4 0.6 bitcast_dynamic-update-slice_fusion.2
  99.9 0.6 bitcast_dynamic-update-slice_fusion.2
  103.3 0.6 bitcast_dynamic-update-slice_fusion.2
  104.6 0.6 bitcast_dynamic-update-slice_fusion.2
  107.4 3.9 %all-to-all-start.3 = ((bf16[32,16,256]{2,1,0:T(8,128)(2,1)}), bf16[32,16,256]{2,1,0:T(8,128)(2,1)S(1)}, u32[]{:S(2)}, u32[]{:S(2)}) async-start(bf16[32,16,256]{2,1,0:T(8,128)(2,1)} %get-tuple-element.29), calls=%async_computation.3 | async-start | bytes 524288 | tf_op jit(solution)/shard_map/all_to_all | solution.py:153
  111.3 0.7 select_reduce_fusion.1
  112.0 0.9 select_reduce_fusion
  112.9 0.9 fusion.33
  113.8 17.4 %all-to-all-done.3 = bf16[32,16,256]{2,1,0:T(8,128)(2,1)S(1)} async-done(((bf16[32,16,256]{2,1,0:T(8,128)(2,1)}), bf16[32,16,256]{2,1,0:T(8,128)(2,1)S(1)}, u32[]{:S(2)}, u32[]{:S(2)}) %all-to-all-start.3) | async-done | bytes 262176 | tf_op jit(solution)/shard_map/all_to_all | solution.py:153
  131.7 0.6 multiply_reduce_fusion
  132.7 4.2 %collective-permute-start = (bf16[1,128,1024]{2,1,0:T(8,128)(2,1)S(1)}, bf16[1,128,1024]{2,1,0:T(8,128)(2,1)S(1)}, u32[]{:S(2)}, u32[]{:S(2)}) collective-permute-start(bf16[1,128,1024]{2,1,0:T(8,128)(2,1)S(1)} %multiply_convert_fusion), channel_id=1, source_target_pairs={{768,0},{0,256},{256,512},{512,768},{769,1},{1,257},{257,513},{513... | collective-permute-start | bytes 786440 | tf_op jit(solution)/shard_map/ppermute | solution.py:59
  136.8 1.9 broadcast_compare_fusion
  138.8 11.5 %collective-permute-done = bf16[1,128,1024]{2,1,0:T(8,128)(2,1)S(1)} collective-permute-done((bf16[1,128,1024]{2,1,0:T(8,128)(2,1)S(1)}, bf16[1,128,1024]{2,1,0:T(8,128)(2,1)S(1)}, u32[]{:S(2)}, u32[]{:S(2)}) %collective-permute-start) | collective-permute-done | bytes 262176 | tf_op jit(solution)/shard_map/ppermute | solution.py:59
  150.2 49.9 %all-gather.2.cloned.1.call-done = bf16[4096,256]{1,0:T(8,128)(2,1)} async-done(((bf16[128,256]{1,0:T(8,128)(2,1)}), bf16[4096,256]{1,0:T(8,128)(2,1)}) %all-gather.2.cloned.1.call-update) | async-done | bytes 2097168 | tf_op jit(solution)/shard_map/all_gather | solution.py:65
  200.2 2.6 %fusion.1 = (f32[4,128]{1,0:T(4,128)S(1)}, f32[4096,128,4]{1,0,2:T(8,128)S(1)}) fusion(pred[128,4096]{0,1:T(8,128)(4,1)S(1)} %broadcast_compare_fusion, bf16[128,4,128]{2,1,0:T(4,128)(2,1)S(1)} %reshape.348, bf16[4096,256]{1,0:T(8,128)(2,1)} %all-gather.2.cloned.1.call-done), kind=kOutput, calls=%fused_computation.6 | convolution fusion | flops 543161856 | bytes 10094592 | tf_op jit(solution)/shard_map/tgqd,kgd->gqtk/dot_general | solution.py:197
  202.8 2.1 fusion.2
  204.9 1.9 fusion.15
  206.9 0.8 copy.54
  207.6 0.7 copy.78
  (116 shorter events, 12.5 us)
Async XLA Ops:
  7.2 4.0 %copy-start = (bf16[1,128,128]{2,1,0:T(8,128)(2,1)S(1)}, bf16[1,128,128]{2,1,0:T(8,128)(2,1)}, u32[]{:S(2)}) copy-start(bf16[1,128,128]{2,1,0:T(8,128)(2,1)} %param.16) | copy-start | bytes 98308
  7.2 124.5 %copy-start.3 = (f32[1,16,128]{2,1,0:T(8,128)S(1)}, f32[1,16,128]{2,1,0:T(8,128)}, u32[]{:S(2)}) copy-start(f32[1,16,128]{2,1,0:T(8,128)} %param.18) | copy-start | bytes 24580
  7.2 124.2 %copy-start.2 = (bf16[1,128,128]{2,1,0:T(8,128)(2,1)S(1)}, bf16[1,128,128]{2,1,0:T(8,128)(2,1)}, u32[]{:S(2)}) copy-start(bf16[1,128,128]{2,1,0:T(8,128)(2,1)} %param.17) | copy-start | bytes 98308
  7.2 124.5 %copy-start.6 = (f32[1,16]{1,0:T(1,128)S(1)}, f32[1,16]{1,0:T(1,128)}, u32[]{:S(2)}) copy-start(f32[1,16]{1,0:T(1,128)} %param.20) | copy-start | bytes 196
  7.2 125.3 %copy-start.4 = (f32[1,1024]{1,0:T(1,128)S(1)}, f32[1,1024]{1,0:T(1,128)}, u32[]{:S(2)}) copy-start(f32[1,1024]{1,0:T(1,128)} %param.21) | copy-start | bytes 12292
  11.1 127.6 %copy-start.1 = (bf16[1,128,512]{2,1,0:T(8,128)(2,1)S(1)}, bf16[1,128,512]{2,1,0:T(8,128)(2,1)}, u32[]{:S(2)}) copy-start(bf16[1,128,512]{2,1,0:T(8,128)(2,1)} %param.22) | copy-start | bytes 393220
  48.8 19.1 %all-to-all-start.2 = ((bf16[32,1,8,256]{3,2,1,0:T(8,128)(2,1)}), bf16[32,1,8,256]{3,2,1,0:T(8,128)(2,1)S(1)}, u32[]{:S(2)}, u32[]{:S(2)}) async-start(bf16[32,1,8,256]{3,2,1,0:T(8,128)(2,1)} %get-tuple-element.67), calls=%async_computation.2 | async-start | bytes 262144 | tf_op jit(solution)/shard_map/all_to_all | solution.py:41
  52.6 147.5 %all-gather.2.cloned.1.call-start = ((), (), s32[]{:S(2)}) async-start(), calls=%async_computation.4 | async-start | bytes 2162688 | tf_op jit(solution)/shard_map/all_gather | solution.py:65
  68.5 17.0 %all-to-all-start = ((f32[32,1,16]{2,1,0:T(1,128)}), f32[32,1,16]{2,1,0:T(1,128)S(1)}, u32[]{:S(2)}, u32[]{:S(2)}) async-start(f32[32,1,16]{2,1,0:T(1,128)} %broadcast_in_dim.108), calls=%async_computation | async-start | bytes 32768 | tf_op jit(solution)/shard_map/all_to_all | solution.py:47
  107.4 23.9 %all-to-all-start.3 = ((bf16[32,16,256]{2,1,0:T(8,128)(2,1)}), bf16[32,16,256]{2,1,0:T(8,128)(2,1)S(1)}, u32[]{:S(2)}, u32[]{:S(2)}) async-start(bf16[32,16,256]{2,1,0:T(8,128)(2,1)} %get-tuple-element.29), calls=%async_computation.3 | async-start | bytes 524288 | tf_op jit(solution)/shard_map/all_to_all | solution.py:153
  132.7 17.6 %collective-permute-start = (bf16[1,128,1024]{2,1,0:T(8,128)(2,1)S(1)}, bf16[1,128,1024]{2,1,0:T(8,128)(2,1)S(1)}, u32[]{:S(2)}, u32[]{:S(2)}) collective-permute-start(bf16[1,128,1024]{2,1,0:T(8,128)(2,1)S(1)} %multiply_convert_fusion), channel_id=1, source_target_pairs={{768,0},{0,256},{256,512},{512,768},{769,1},{1,257},{257,513},{513... | collective-permute-start | bytes 786440 | tf_op jit(solution)/shard_map/ppermute | solution.py:59
  200.2 4.7 %copy-start.5 = (bf16[4096,256]{1,0:T(8,128)(2,1)S(1)}, bf16[4096,256]{1,0:T(8,128)(2,1)}, u32[]{:S(2)}) copy-start(bf16[4096,256]{1,0:T(8,128)(2,1)} %all-gather.2.cloned.1.call-done) | copy-start | bytes 6291460
Sparse Core Ops, SparseCore 0:
  56.1 143.9 all-gather.1
where the time goes:
time: 217 us; the launch traced here: 215 us
  waiting for transfers between devices  105 us (48%)
  blocking collectives  36.3 us (17%)
  other arithmetic  31.7 us (15%)
  starting transfers between devices  15.8 us (7%)
  between operations  14.4 us (7%)
  matrix products  6.53 us (3%)
  local copies, waits for them, and re-layouts  5.93 us (3%)
    all_gather x1, waiting for transfers between devices, sent_together(): filled = lax.all_gather(both, axis, axis=dim, tiled=True)  49.9 us
    all_to_all x1, blocking collectives, exchange_in_pieces(): lax.all_to_all(share, axis, split_axis=0, concat_axis=0, tiled=True)  36.3 us
    dynamic_update_slice x32, other arithmetic, shards(): lax.scan(prefix_step, jnp.zeros_like(slices_in[0]), (all_totals, slices_in))  19.3 us
    all_to_all x1, waiting for transfers between devices, shards(): lax.all_to_all(prefixed.astype(jnp.bfloat16), 'ctx', split_axis=0, concat...  17.4 us
    all_to_all x1, waiting for transfers between devices, from_everyone(): lax.all_to_all(jnp.broadcast_to(array[None], (devices, *array.shape)), ax...  13.1 us
    all_to_all x1, waiting for transfers between devices, exchange_in_pieces(): lax.all_to_all(share, axis, split_axis=0, concat_axis=0, tiled=True)  12.6 us
    ppermute x1, waiting for transfers between devices, passed_along(): return lax.ppermute(block, axis, route)  11.5 us
  transfers between devices with their start and end apart: 5, of which 5 were waited for; matrix products, arithmetic and copies ran while one was open for 14% of the time, Pallas kernels for 0%

commit v1 on v0

v1 whole, which is shorter than its diff:
```python
import functools
import math

import jax
import jax.numpy as jnp
from jax import lax
from jax.experimental import pallas as pl
from jax.experimental.pallas import tpu as pltpu
from jax.sharding import PartitionSpec as P

MESH = pl.DeviceIdType.MESH
F32 = jnp.float32
BF16 = jnp.bfloat16
HIGH = lax.Precision.HIGHEST
NEG = -1e30
TOK = 128
HALF = 64
HEADS = 16
HEADP = 64
FEAT = HEADS * HEADP
TILES = FEAT // 128
OWN = TILES // 2
QH = 4
SCALE2 = math.log2(math.e) / math.sqrt(128.0)


def contract(a, b, da, db, precision=None):
    return lax.dot_general(
        a, b, (((da,), (db,)), ((), ())), precision=precision, preferred_element_type=F32
    )


def kernel(
    nz,
    nsec,
    x_ref,
    gate_ref,
    b_ref,
    c_ref,
    step_ref,
    rate_ref,
    skip_ref,
    gain_ref,
    q_ref,
    k_ref,
    v_ref,
    order_ref,
    hand_ref,
    att_ref,
    kv,
    qall,
    peak,
    den,
    acc,
    ecum,
    rhs,
    lhs,
    drow,
    ctile,
    crecv,
    drecv,
    dpair,
    pbuf,
    arecv,
    adec,
    pref,
    sin,
    ssend,
    gated,
    mixed,
    osend,
    orecv,
    stsend,
    strecv,
    kv_ss,
    kv_rs,
    y_ss,
    y_rs,
    a_ss,
    a_rs,
    ad_ss,
    ad_rs,
    r_ss,
    r_rs,
    h_ss,
    h_rs,
):
    sec = lax.axis_index("section")
    ctx = lax.axis_index("ctx")
    z = ctx // 2
    y = ctx % 2
    half = nz // 2
    rows = OWN * TOK // nz
    partner = {"ctx": z * 2 + 1 - y}

    def at_z(k):
        return {"ctx": k * 2 + y}

    def around(k):
        return lax.rem(k + nz, nz)

    following = {"section": lax.rem(sec + 1, nsec)}
    previous = {"section": lax.rem(sec + nsec - 1, nsec)}

    def copy(src, dst, ss, rs, to):
        return pltpu.make_async_remote_copy(
            src_ref=src, dst_ref=dst, send_sem=ss, recv_sem=rs, device_id=to, device_id_type=MESH
        )

    sent = []

    def start(c):
        c.start()
        sent.append(c)

    barrier = pltpu.get_barrier_semaphore()
    for o in range(1, nz):
        pl.semaphore_signal(barrier, inc=1, device_id=at_z(around(z + o)), device_id_type=MESH)
    for to in (partner, following, previous):
        pl.semaphore_signal(barrier, inc=1, device_id=to, device_id_type=MESH)

    kv[z, 0] = k_ref[...]
    kv[z, 1] = v_ref[...]
    for h in range(QH):
        qall[h * TOK : (h + 1) * TOK] = q_ref[:, h * 128 : (h + 1) * 128]
    pl.semaphore_wait(barrier, nz - 1 + 3)

    def ring_copy(way, s, t, arriving):
        if way == 0:
            slot, to = (around(z - s), z) if arriving else (around(z - s + 1), around(z + 1))
        else:
            slot, to = (around(z + s), z) if arriving else (around(z + s - 1), around(z - 1))
        if arriving:
            to = around(z + 1)
        place = kv.at[slot, t]
        return copy(place, place, kv_ss.at[way, s, t], kv_rs.at[way, s, t], at_z(to))

    def ring_parts(s):
        if s < half:
            return [(w, t) for t in (0, 1) for w in (0, 1)]
        return [(0, 0), (1, 1)]

    def ring_send(s):
        for w, t in ring_parts(s):
            start(ring_copy(w, s, t, False))

    def ring_hop(s):
        going = ring_parts(s + 1) if s < half else []
        for w, t in ring_parts(s):
            ring_copy(w, s, t, True).wait_recv()
            if (w, t) in going:
                start(ring_copy(w, s + 1, t, False))

    ring_send(1)
    start(copy(qall.at[pl.ds(0, QH * TOK)], qall.at[pl.ds(QH * TOK, QH * TOK)], y_ss.at[0], y_rs.at[0], partner))

    row16 = lax.broadcasted_iota(jnp.int32, (HEADS, TOK), 0)
    rate = jnp.zeros((HEADS, TOK), F32)
    for h in range(HEADS):
        rate = jnp.where(row16 == h, rate_ref[0, h], rate)
    row = lax.broadcasted_iota(jnp.int32, (TOK, 128), 0)
    lane = lax.broadcasted_iota(jnp.int32, (TOK, 128), 1)
    step = step_ref[...]
    upper = jnp.where(row <= lane, 1.0, 0.0).astype(F32)
    cum = contract(-rate * step, upper, 1, 0, HIGH)
    scales = jnp.concatenate([jnp.exp(cum), jnp.exp(-cum) * step], axis=1)
    head_of = lax.shift_right_logical(lax.broadcasted_iota(jnp.int32, (HEADS, FEAT), 1), 6)
    spread = jnp.where(head_of == lax.broadcasted_iota(jnp.int32, (HEADS, FEAT), 0), 1.0, 0.0)
    for j in range(TILES):
        cols = slice(j * 128, (j + 1) * 128)
        wide = contract(scales, spread[:, cols], 0, 0, HIGH)
        ecum[:, cols] = wide[:TOK]
        drow[j] = wide[TOK - 1 : TOK]
        xf = (x_ref[:, cols].astype(F32) * wide[TOK:]).astype(BF16)
        rhs[j, 0:TOK] = xf
        ctile[j] = (contract(b_ref[...], xf, 0, 0) * wide[TOK - 1 : TOK]).astype(BF16)
    theirs = (1 - y) * OWN
    mine = y * OWN
    start(copy(drow.at[pl.ds(theirs, OWN)], drecv, y_ss.at[1], y_rs.at[1], partner))
    for c in range(OWN):
        start(copy(ctile.at[theirs + c], crecv.at[c], y_ss.at[2 + c], y_rs.at[2 + c], partner))
    inner = contract(c_ref[...], b_ref[...], 1, 1)
    lhs[:, 0:TOK] = jnp.where(lane <= row, inner, 0.0).astype(BF16)
    lhs[:, TOK:] = c_ref[...]

    row_in = jnp.bitwise_and(row, HALF - 1)
    lane1 = lax.broadcasted_iota(jnp.int32, (1, 128), 1)

    def query_pos(at):
        o0 = order_ref[0, 2 * at]
        o1 = order_ref[0, 2 * at + 1]
        return jnp.where(lane1 < HALF, o0, o1) * HALF + jnp.bitwise_and(lane1, HALF - 1)

    qpos = [query_pos(ctx), query_pos(z * 2 + 1 - y)]
    peak[...] = jnp.full(peak.shape, NEG, F32)
    den[...] = jnp.zeros(den.shape, F32)
    acc[...] = jnp.zeros(acc.shape, F32)

    def attend(slots):
        biases = []
        for slot in slots:
            at = slot * 2 + y
            o0 = order_ref[0, 2 * at]
            o1 = order_ref[0, 2 * at + 1]
            kpos = jnp.where(row < HALF, o0, o1) * HALF + row_in
            biases.append([jnp.where(kpos <= p, 0.0, NEG).astype(F32) for p in qpos])
        keys = jnp.concatenate([kv[s, 0] for s in slots], axis=0)
        values = jnp.concatenate([kv[s, 1] for s in slots], axis=0)
        for src in range(2):
            bias = jnp.concatenate([b[src] for b in biases], axis=0)
            bias = jnp.concatenate([bias, bias], axis=1)
            for pair in range(QH // 2):
                cols = slice(src * QH * TOK + pair * 256, src * QH * TOK + (pair + 1) * 256)
                scores = contract(keys, qall[cols], 1, 1) + bias
                old = peak[:, cols]
                new = jnp.maximum(old, jnp.max(scores, axis=0, keepdims=True))
                weights = jnp.exp2((scores - new) * SCALE2)
                fade = jnp.exp2((old - new) * SCALE2)
                peak[:, cols] = new
                den[:, cols] = den[:, cols] * fade + jnp.sum(weights, axis=0, keepdims=True)
                acc[:, cols] = acc[:, cols] * fade + contract(values, weights.astype(BF16), 0, 0)

    def attend_step(s):
        if s < half:
            attend([around(z - s), around(z + s)])
        else:
            attend([around(z - s)])

    hops = iter(range(1, half + 1))
    steps = iter(range(1, half + 1))

    def hop(n):
        for _ in range(n):
            s = next(hops, None)
            if s is not None:
                ring_hop(s)

    def work(n):
        for _ in range(n):
            s = next(steps, None)
            if s is not None:
                attend_step(s)

    copy(qall.at[pl.ds(0, QH * TOK)], qall.at[pl.ds(QH * TOK, QH * TOK)], y_ss.at[0], y_rs.at[0], partner).wait_recv()
    hop(1)
    attend([z])

    yf = y.astype(F32)
    copy(drow.at[pl.ds(theirs, OWN)], drecv, y_ss.at[1], y_rs.at[1], partner).wait_recv()
    for c in range(OWN):
        copy(ctile.at[theirs + c], crecv.at[c], y_ss.at[2 + c], y_rs.at[2 + c], partner).wait_recv()
        d_mine = drow[mine + c]
        d_other = drecv[c]
        dpair[c] = d_mine * d_other
        a = d_other * (1.0 - yf) + yf
        b = d_mine * yf + (1.0 - yf)
        total = ctile[mine + c].astype(F32) * a + crecv[c].astype(F32) * b
        for r in range(TOK // rows):
            pbuf[c * (TOK // rows) + r] = total[r * rows : (r + 1) * rows].astype(BF16)
    per_tile = TOK // rows
    far_first = sorted(range(1, nz), key=lambda o: -min(o, nz - o))
    for o in far_first:
        k = around(z + o)
        start(copy(dpair.at[k // per_tile], adec.at[z], ad_ss.at[o], ad_rs.at[z], at_z(k)))
        start(copy(pbuf.at[k], arecv.at[z], a_ss.at[o], a_rs.at[z], at_z(k)))
    arecv[z] = pbuf[z]
    adec[z] = dpair[z // per_tile]

    hop(1)
    work(1)
    hop(1)
    work(1)

    for o in range(1, nz):
        k = around(z + o)
        copy(dpair.at[0], adec.at[k], ad_ss.at[o], ad_rs.at[k], at_z(k)).wait_recv()
        copy(pbuf.at[k], arecv.at[k], a_ss.at[o], a_rs.at[k], at_z(k)).wait_recv()
    state = jnp.zeros((rows, 128), F32)
    for k in range(nz):
        pref[k] = state.astype(BF16)
        state = adec[k] * state + arecv[k].astype(F32)
    for o in far_first:
        k = around(z + o)
        start(copy(pref.at[k], sin.at[z], r_ss.at[o], r_rs.at[z], at_z(k)))
    sin[z] = pref[z]

    hop(1)
    work(1)
    hop(1)
    work(1)

    for o in range(1, nz):
        k = around(z + o)
        copy(pref.at[k], sin.at[k], r_ss.at[o], r_rs.at[k], at_z(k)).wait_recv()
    for c in range(OWN):
        first = jnp.concatenate([sin[c * per_tile + r] for r in range(per_tile)], axis=0).astype(F32)
        d_mine = drow[mine + c]
        d_other = drecv[c]
        d0 = d_mine * (1.0 - yf) + d_other * yf
        c0 = ctile[mine + c].astype(F32) * (1.0 - yf) + crecv[c].astype(F32) * yf
        second = d0 * first + c0
        ssend[c] = (second * (1.0 - yf) + first * yf).astype(BF16)
        place = rhs.at[mine + c, pl.ds(TOK, 128)]
        start(copy(ssend.at[c], place, y_ss.at[2 + OWN + c], y_rs.at[2 + OWN + c], partner))
        rhs[mine + c, TOK:] = (first * (1.0 - yf) + second * yf).astype(BF16)

    hop(1)
    work(1)
    hop(1)
    work(1)

    for c in range(OWN):
        place = rhs.at[theirs + c, pl.ds(TOK, 128)]
        copy(ssend.at[c], place, y_ss.at[2 + OWN + c], y_rs.at[2 + OWN + c], partner).wait_recv()
    squares = jnp.zeros((TOK, 128), F32)
    for j in range(TILES):
        cols = slice(j * 128, (j + 1) * 128)
        skip = jnp.where(lane1 < HEADP, skip_ref[0, 2 * j], skip_ref[0, 2 * j + 1])
        out = ecum[:, cols] * contract(lhs[...], rhs[j], 1, 0) + skip * x_ref[:, cols].astype(F32)
        gate = gate_ref[:, cols].astype(F32)
        value = out * (gate / (1.0 + jnp.exp(-gate)))
        gated[:, cols] = value
        squares += value * value
    factor = lax.rsqrt(jnp.sum(squares, axis=1, keepdims=True) * (1.0 / FEAT) + 1e-5)
    parts = 4
    span = TOK // parts
    for p in range(parts):
        at = slice(p * span, (p + 1) * span)
        mixed[at] = (gated[at] * factor[at] * gain_ref[...]).astype(BF16)
        place = pl.ds(p * span, span)
        start(copy(mixed.at[place], hand_ref.at[place], h_ss.at[p], h_rs.at[p], following))

    hop(half)
    work(half)

    mine_cols = slice(0, QH * TOK)
    other_cols = slice(QH * TOK, 2 * QH * TOK)
    osend[...] = (acc[:, other_cols] / den[:, other_cols]).astype(BF16)
    stsend[0] = peak[:, other_cols]
    stsend[1] = den[:, other_cols]
    swap = copy(osend, orecv, y_ss.at[2 + 2 * OWN], y_rs.at[2 + 2 * OWN], partner)
    swap_stats = copy(stsend, strecv, y_ss.at[3 + 2 * OWN], y_rs.at[3 + 2 * OWN], partner)
    start(swap_stats)
    start(swap)
    swap_stats.wait_recv()
    swap.wait_recv()
    m1 = peak[:, mine_cols]
    m2 = strecv[0]
    top = jnp.maximum(m1, m2)
    w1 = jnp.exp2((m1 - top) * SCALE2)
    w2 = jnp.exp2((m2 - top) * SCALE2) * strecv[1]
    inv = 1.0 / (w1 * den[:, mine_cols] + w2)
    w1 = w1 * inv
    w2 = w2 * inv
    for h in range(QH):
        cols = slice(h * TOK, (h + 1) * TOK)
        both = acc[:, cols] * w1[:, cols] + orecv[:, cols].astype(F32) * w2[:, cols]
        att_ref[:, cols] = both.T.astype(BF16)

    for p in range(parts):
        place = pl.ds(p * span, span)
        copy(mixed.at[place], hand_ref.at[place], h_ss.at[p], h_rs.at[p], following).wait_recv()
    for c in sent:
        c.wait_send()


def shards(nz, nsec, *args):
    flat = [a.reshape(a.shape[1:]) if a.ndim == 3 else a for a in args]
    rows = OWN * TOK // nz
    half = nz // 2
    vmem = pl.BlockSpec(memory_space=pltpu.VMEM)
    smem = pl.BlockSpec(memory_space=pltpu.SMEM)
    in_specs = [vmem] * 5 + [smem, smem] + [vmem] * 4 + [smem]
    dma = pltpu.SemaphoreType.DMA
    swaps = 4 + 2 * OWN
    handed, attended = pl.pallas_call(
        functools.partial(kernel, nz, nsec),
        out_shape=(
            jax.ShapeDtypeStruct((TOK, FEAT), BF16),
            jax.ShapeDtypeStruct((TOK, QH * 128), BF16),
        ),
        in_specs=in_specs,
        out_specs=(vmem, vmem),
        scratch_shapes=[
            pltpu.VMEM((nz, 2, TOK, 128), BF16),
            pltpu.VMEM((2 * QH * TOK, 128), BF16),
            pltpu.VMEM((1, 2 * QH * TOK), F32),
            pltpu.VMEM((1, 2 * QH * TOK), F32),
            pltpu.VMEM((128, 2 * QH * TOK), F32),
            pltpu.VMEM((TOK, FEAT), F32),
            pltpu.VMEM((TILES, TOK + 128, 128), BF16),
            pltpu.VMEM((TOK, TOK + 128), BF16),
            pltpu.VMEM((TILES, 1, 128), F32),
            pltpu.VMEM((TILES, 128, 128), BF16),
            pltpu.VMEM((OWN, 128, 128), BF16),
            pltpu.VMEM((OWN, 1, 128), F32),
            pltpu.VMEM((OWN, 1, 128), F32),
            pltpu.VMEM((nz, rows, 128), BF16),
            pltpu.VMEM((nz, rows, 128), BF16),
            pltpu.VMEM((nz, 1, 128), F32),
            pltpu.VMEM((nz, rows, 128), BF16),
            pltpu.VMEM((nz, rows, 128), BF16),
            pltpu.VMEM((OWN, 128, 128), BF16),
            pltpu.VMEM((TOK, FEAT), F32),
            pltpu.VMEM((TOK, FEAT), BF16),
            pltpu.VMEM((128, QH * TOK), BF16),
            pltpu.VMEM((128, QH * TOK), BF16),
            pltpu.VMEM((2, 1, QH * TOK), F32),
            pltpu.VMEM((2, 1, QH * TOK), F32),
            dma((2, half + 1, 2)),
            dma((2, half + 1, 2)),
            dma((swaps,)),
            dma((swaps,)),
            dma((nz,)),
            dma((nz,)),
            dma((nz,)),
            dma((nz,)),
            dma((nz,)),
            dma((nz,)),
            dma((4,)),
            dma((4,)),
        ],
        compiler_params=pltpu.CompilerParams(
            collective_id=0, has_side_effects=True, vmem_limit_bytes=32 * 1024 * 1024
        ),
        cost_estimate=pl.CostEstimate(
            flops=1300000000, bytes_accessed=1400000, transcendentals=2500000
        ),
    )(*flat)
    return handed[None], attended[None]


def solution(mesh):
    nz = mesh.shape["ctx"] // 2
    nsec = mesh.shape["section"]
    wide = P("section", "ctx", "tp")
    return jax.shard_map(
        functools.partial(shards, nz, nsec),
        mesh=mesh,
        in_specs=(
            wide,
            wide,
            wide,
            wide,
            P("section", "tp", "ctx"),
            P("section", "tp"),
            P("section", "tp"),
            P("section", "tp"),
            wide,
            wide,
            wide,
            P("section", None),
        ),
        out_specs=(wide, wide),
        check_vma=False,
    )
```

time: 217 us -> 80.7 us (0.37)
  waiting for transfers between devices: 105 us -> 0 us
  Pallas kernels: 0 us -> 71.6 us
  blocking collectives: 36.3 us -> 0 us
  other arithmetic: 31.7 us -> 0 us
  starting transfers between devices: 15.8 us -> 0 us
  between operations: 14.4 us -> 0.69 us
  matrix products: 6.53 us -> 0 us
    pallas_call x0 -> x1, Pallas kernels: none -> 71.6 us  [shards(): pl.pallas_call(functools.partial(kernel, nz, nsec), out_shape=(jax.ShapeD...]
    all_gather x1 -> x0, waiting for transfers between devices: 49.9 us -> none  [sent_together(): filled = lax.all_gather(both, axis, axis=dim, tiled=True)]
    all_to_all x3 -> x0, waiting for transfers between devices: 43.2 us -> none  [the longest x1 17.4 us: shards(): lax.all_to_all(prefixed.astype(jnp.bfloat16), 'ctx', split_axis=0, concat...]
    all_to_all x1 -> x0, blocking collectives: 36.3 us -> none  [exchange_in_pieces(): lax.all_to_all(share, axis, split_axis=0, concat_axis=0, tiled=True)]
    dynamic_update_slice x32 -> x0, other arithmetic: 19.3 us -> none  [shards(): lax.scan(prefix_step, jnp.zeros_like(slices_in[0]), (all_totals, slices_in))]
    all_to_all x3 -> x0, starting transfers between devices: 11.6 us -> none  [the longest x1 3.87 us: shards(): lax.all_to_all(prefixed.astype(jnp.bfloat16), 'ctx', split_axis=0, concat...]
    ppermute x1 -> x0, waiting for transfers between devices: 11.5 us -> none  [passed_along(): return lax.ppermute(block, axis, route)]
    dot_general x6 -> x0, matrix products: 6.53 us -> none  [the longest x1 2.63 us: shards(): jnp.einsum('tgqd,kgd->gqtk', query_rows, key_heads, preferred_element_typ...]
  transfers between devices with their start and end apart: 5 -> 0, of which waited for: 5 -> 0; matrix products, arithmetic and copies ran while one was open for 14% -> 0% of each run, Pallas kernels for 0% -> 0%
where the time goes in v1:
time: 80.7 us; the launch traced here: 80.2 us
  Pallas kernels  71.6 us (89%)
  local copies, waits for them, and re-layouts  7.87 us (10%)
    pallas_call x1, Pallas kernels, shards(): pl.pallas_call(functools.partial(kernel, nz, nsec), out_shape=(jax.ShapeD...  71.6 us
    unnamed x26, local copies, waits for them, and re-layouts  7.87 us

profile of v1, /device:TPU:6, one launch (start us, length us, event | category | flops | bytes accessed | tf_op | source)
XLA Modules:
  0.0 80.2 jit_solution(2130654480120071664)
XLA Ops:
  0.6 0.0 copy-start.7
  0.6 0.0 copy-start.8
  0.7 0.0 copy-start.9
  0.7 0.0 copy-start.10
  0.7 0.0 copy-start.11
  0.7 0.6 copy-done.7
  1.3 0.0 copy-done.8
  1.3 0.0 copy-done.9
  1.3 0.0 copy-done.10
  1.3 0.0 copy-done.11
  1.4 0.0 copy-start
  1.4 0.9 %copy-done = bf16[1,128,1024]{2,1,0:T(8,128)(2,1)S(1)} copy-done((bf16[1,128,1024]{2,1,0:T(8,128)(2,1)S(1)}, bf16[1,128,1024]{2,1,0:T(8,128)(2,1)}, u32[]{:S(2)}) %copy-start) | copy-done | bytes 262168
  2.3 0.0 copy-start.1
  2.3 0.9 %copy-done.1 = bf16[1,128,1024]{2,1,0:T(8,128)(2,1)S(1)} copy-done((bf16[1,128,1024]{2,1,0:T(8,128)(2,1)S(1)}, bf16[1,128,1024]{2,1,0:T(8,128)(2,1)}, u32[]{:S(2)}) %copy-start.1) | copy-done | bytes 262168
  3.3 0.0 copy-start.2
  3.3 0.9 %copy-done.2 = bf16[1,128,512]{2,1,0:T(8,128)(2,1)S(1)} copy-done((bf16[1,128,512]{2,1,0:T(8,128)(2,1)S(1)}, bf16[1,128,512]{2,1,0:T(8,128)(2,1)}, u32[]{:S(2)}) %copy-start.2) | copy-done | bytes 131096
  4.2 0.0 copy-start.3
  4.2 0.8 copy-done.3
  4.9 0.0 copy-start.4
  4.9 0.8 copy-done.4
  5.7 0.0 copy-start.5
  5.7 0.8 copy-done.5
  6.4 0.0 copy-start.6
  6.4 0.8 copy-done.6
  7.2 71.6 %shard_map.131 = (bf16[128,1024]{1,0:T(8,128)(2,1)S(1)}, bf16[128,512]{1,0:T(8,128)(2,1)S(1)}) custom-call(bf16[128,1024]{1,0:T(8,128)(2,1)S(1)} %bitcast.12, bf16[128,1024]{1,0:T(8,128)(2,1)S(1)} %bitcast.13, bf16[128,128]{1,0:T(8,128)(2,1)S(1)} %bitcast.15, bf16[128,128]{1,0:T(8,128)(2,1)S(1)} %bitcast.16, f32[16,128]{1,0:T(8,128)S(1)} %bitcast.19, ...), custom_call_target="tpu_custom_call" | custom-call | flops 1300000000 | bytes 1400000 | tf_op jit(solution)/shard_map/pallas_call | solution.py:376
  78.8 0.7 copy.16
  79.5 0.7 copy.17
Async XLA Ops:
  0.6 0.7 copy-start.7
  0.6 0.7 copy-start.8
  0.7 0.7 copy-start.9
  0.7 0.7 copy-start.10
  0.7 0.7 copy-start.11
  1.4 0.9 %copy-start = (bf16[1,128,1024]{2,1,0:T(8,128)(2,1)S(1)}, bf16[1,128,1024]{2,1,0:T(8,128)(2,1)}, u32[]{:S(2)}) copy-start(bf16[1,128,1024]{2,1,0:T(8,128)(2,1)} %param.12) | copy-start | bytes 786436
  2.3 0.9 %copy-start.1 = (bf16[1,128,1024]{2,1,0:T(8,128)(2,1)S(1)}, bf16[1,128,1024]{2,1,0:T(8,128)(2,1)}, u32[]{:S(2)}) copy-start(bf16[1,128,1024]{2,1,0:T(8,128)(2,1)} %param.13) | copy-start | bytes 786436
  3.3 0.9 %copy-start.2 = (bf16[1,128,512]{2,1,0:T(8,128)(2,1)S(1)}, bf16[1,128,512]{2,1,0:T(8,128)(2,1)}, u32[]{:S(2)}) copy-start(bf16[1,128,512]{2,1,0:T(8,128)(2,1)} %param.20) | copy-start | bytes 393220
  4.2 0.8 copy-start.3
  4.9 0.8 copy-start.4
  5.7 0.8 copy-start.5
  6.4 0.8 copy-start.6

commit v2 on v1

v2 whole, which is shorter than its diff:
```python
import functools
import math

import jax
import jax.numpy as jnp
from jax import lax
from jax.experimental import pallas as pl
from jax.experimental.pallas import tpu as pltpu
from jax.sharding import PartitionSpec as P

MESH = pl.DeviceIdType.MESH
F32 = jnp.float32
BF16 = jnp.bfloat16
HIGH = lax.Precision.HIGHEST
NEG = -1e30
TOK = 128
HALF = 64
HEADS = 16
HEADP = 64
FEAT = HEADS * HEADP
TILES = FEAT // 128
OWN = TILES // 2
QH = 4
SCALE2 = math.log2(math.e) / math.sqrt(128.0)


def contract(a, b, da, db, precision=None):
    return lax.dot_general(
        a, b, (((da,), (db,)), ((), ())), precision=precision, preferred_element_type=F32
    )


def kernel(
    nz,
    nsec,
    x_in,
    gate_in,
    b_in,
    c_in,
    step_in,
    rate_in,
    skip_in,
    gain_in,
    q_in,
    k_in,
    v_in,
    order_in,
    hand_ref,
    att_ref,
    xs,
    gates,
    writes,
    reads,
    steps,
    rate_ref,
    skip_ref,
    gain_ref,
    order_ref,
    kv,
    qall,
    peak,
    den,
    acc,
    ecum,
    rhs,
    lhs,
    drow,
    cstate,
    dpair,
    pbuf,
    arecv,
    adec,
    pref,
    sin,
    ubuf,
    hrecv,
    sqsend,
    sqrecv,
    osend,
    orecv,
    stsend,
    strecv,
    kv_ss,
    kv_rs,
    y_ss,
    y_rs,
    a_ss,
    a_rs,
    ad_ss,
    ad_rs,
    r_ss,
    r_rs,
    h_ss,
    h_rs,
    in_s,
):
    sec = lax.axis_index("section")
    ctx = lax.axis_index("ctx")
    z = ctx // 2
    y = ctx % 2
    half = nz // 2
    rows = OWN * TOK // nz
    per_tile = TOK // rows
    wide = OWN * 128
    partner = {"ctx": z * 2 + 1 - y}

    def at_z(k):
        return {"ctx": k * 2 + y}

    def around(k):
        return lax.rem(k + nz, nz)

    def in_section(i, t):
        return {"section": lax.rem(sec + i, nsec), "ctx": z * 2 + t}

    def copy(src, dst, ss, rs, to):
        return pltpu.make_async_remote_copy(
            src_ref=src, dst_ref=dst, send_sem=ss, recv_sem=rs, device_id=to, device_id_type=MESH
        )

    sent = []

    def start(c):
        c.start()
        sent.append(c)

    mine = pl.ds(pl.multiple_of(y * wide, 128), wide)

    def theirs(start_at, width):
        return pl.ds(pl.multiple_of((1 - y) * wide + start_at, 128), width)

    fetches = [
        (step_in, steps.at[y]),
        (rate_in, rate_ref),
        (x_in.at[:, mine], xs.at[y]),
        (b_in, writes.at[y]),
        (k_in, kv.at[z, 0]),
        (v_in, kv.at[z, 1]),
        (c_in, reads.at[y]),
        (q_in.at[:, 0:128], qall.at[0:TOK]),
        (q_in.at[:, 128:256], qall.at[TOK : 2 * TOK]),
        (q_in.at[:, 256:384], qall.at[2 * TOK : 3 * TOK]),
        (q_in.at[:, 384:512], qall.at[3 * TOK : 4 * TOK]),
        (order_in, order_ref),
        (gate_in.at[:, mine], gates.at[y]),
        (skip_in, skip_ref),
        (gain_in.at[:, mine], gain_ref),
    ]
    fetches = [pltpu.make_async_copy(s, d, in_s.at[i]) for i, (s, d) in enumerate(fetches)]

    barrier = pltpu.get_barrier_semaphore()
    for o in range(1, nz):
        pl.semaphore_signal(barrier, inc=1, device_id=at_z(around(z + o)), device_id_type=MESH)
    for to in (
        partner,
        in_section(1, 0),
        in_section(1, 1),
        in_section(nsec - 1, 0),
        in_section(nsec - 1, 1),
    ):
        pl.semaphore_signal(barrier, inc=1, device_id=to, device_id_type=MESH)
    for f in fetches:
        f.start()
    pl.semaphore_wait(barrier, nz - 1 + 5)

    hw = wide // 2
    give_steps = copy(step_in, steps.at[y], y_ss.at[0], y_rs.at[0], partner)
    give_b = copy(b_in, writes.at[y], y_ss.at[1], y_rs.at[1], partner)
    give_x = [
        copy(
            x_in.at[:, theirs(i * hw, hw)],
            xs.at[y, :, i * hw : (i + 1) * hw],
            y_ss.at[2 + i],
            y_rs.at[2 + i],
            partner,
        )
        for i in range(2)
    ]
    give_c = copy(c_in, reads.at[y], y_ss.at[4], y_rs.at[4], partner)
    give_gate = copy(gate_in.at[:, theirs(0, wide)], gates.at[y], y_ss.at[5], y_rs.at[5], partner)
    give_q = copy(
        qall.at[pl.ds(0, QH * TOK)], qall.at[pl.ds(QH * TOK, QH * TOK)], y_ss.at[6], y_rs.at[6], partner
    )
    for c in (give_steps, give_b, *give_x):
        start(c)

    def ring_copy(way, s, t, arriving):
        if way == 0:
            slot, to = around(z - s + (0 if arriving else 1)), around(z + 1)
        else:
            slot, to = around(z + s - (0 if arriving else 1)), around(z - 1)
        place = kv.at[slot, t]
        return copy(place, place, kv_ss.at[way, s, t], kv_rs.at[way, s, t], at_z(to))

    def ring_parts(s):
        if s < half:
            return [(w, t) for t in (0, 1) for w in (0, 1)]
        return [(0, 0), (1, 1)]

    def ring_hop(s):
        going = ring_parts(s + 1) if s < half else []
        for w, t in ring_parts(s):
            ring_copy(w, s, t, True).wait_recv()
            if (w, t) in going:
                start(ring_copy(w, s + 1, t, False))

    for f in fetches[:6]:
        f.wait()
    for w, t in ring_parts(1):
        start(ring_copy(w, 1, t, False))
    row16 = lax.broadcasted_iota(jnp.int32, (HEADS, TOK), 0)
    rate = jnp.zeros((HEADS, TOK), F32)
    for h in range(HEADS):
        rate = jnp.where(row16 == h, rate_ref[0, h], rate)
    row = lax.broadcasted_iota(jnp.int32, (TOK, 128), 0)
    lane = lax.broadcasted_iota(jnp.int32, (TOK, 128), 1)
    upper = jnp.where(row <= lane, 1.0, 0.0).astype(F32)
    lane_head = lax.shift_right_logical(lane[:HEADS], 6)

    def scales_of(t):
        step = steps[t]
        cum = contract(-rate * step, upper, 1, 0, HIGH)
        return jnp.concatenate([jnp.exp(cum), jnp.exp(-cum) * step], axis=1)

    def block_tile(t, scales, c):
        cols = slice(c * 128, (c + 1) * 128)
        spread = jnp.where(row16 - y * (2 * OWN) - 2 * c == lane_head, 1.0, 0.0).astype(F32)
        spread_out = contract(scales, spread, 0, 0, HIGH)
        ecum[t, c] = spread_out[:TOK]
        d = spread_out[TOK - 1 : TOK]
        drow[t, c] = d
        xf = (xs[t, :, cols].astype(F32) * spread_out[TOK:]).astype(BF16)
        rhs[t, c, 0:TOK] = xf
        cstate[t, c] = contract(writes[t], xf, 0, 0) * d

    def block_lhs(t):
        inner = contract(reads[t], writes[t], 1, 1)
        lhs[t, :, 0:TOK] = jnp.where(lane <= row, inner, 0.0).astype(BF16)
        lhs[t, :, TOK:] = reads[t]

    scales = scales_of(y)
    for c in range(OWN):
        block_tile(y, scales, c)
    for f in fetches[6:]:
        f.wait()
    start(give_c)
    start(give_q)
    start(give_gate)
    give_steps.wait_recv()
    give_b.wait_recv()
    scales = scales_of(1 - y)
    for c in range(OWN):
        if c % (OWN // 2) == 0:
            give_x[c // (OWN // 2)].wait_recv()
        block_tile(1 - y, scales, c)
        d1 = drow[1, c]
        dpair[c] = drow[0, c] * d1
        total = cstate[0, c] * d1 + cstate[1, c]
        for r in range(per_tile):
            pbuf[c * per_tile + r] = total[r * rows : (r + 1) * rows].astype(BF16)
    far_first = sorted(range(1, nz), key=lambda o: -min(o, nz - o))
    for o in far_first:
        k = around(z + o)
        start(copy(dpair.at[k // per_tile], adec.at[z], ad_ss.at[o], ad_rs.at[z], at_z(k)))
        start(copy(pbuf.at[k], arecv.at[z], a_ss.at[o], a_rs.at[z], at_z(k)))
    arecv[z] = pbuf[z]
    adec[z] = dpair[z // per_tile]

    row_in = jnp.bitwise_and(row, HALF - 1)
    lane1 = lax.broadcasted_iota(jnp.int32, (1, 128), 1)

    def query_pos(at):
        o0 = order_ref[0, 2 * at]
        o1 = order_ref[0, 2 * at + 1]
        return jnp.where(lane1 < HALF, o0, o1) * HALF + jnp.bitwise_and(lane1, HALF - 1)

    qpos = [query_pos(ctx), query_pos(z * 2 + 1 - y)]

    def attend(slots, first=False):
        biases = []
        for slot in slots:
            at = slot * 2 + y
            o0 = order_ref[0, 2 * at]
            o1 = order_ref[0, 2 * at + 1]
            kpos = jnp.where(row < HALF, o0, o1) * HALF + row_in
            biases.append([jnp.where(kpos <= p, 0.0, NEG).astype(F32) for p in qpos])
        keys = jnp.concatenate([kv[s, 0] for s in slots], axis=0)
        values = jnp.concatenate([kv[s, 1] for s in slots], axis=0)
        for src in range(2):
            bias = jnp.concatenate([b[src] for b in biases], axis=0)
            bias = jnp.concatenate([bias, bias], axis=1)
            for pair in range(QH // 2):
                cols = slice(src * QH * TOK + pair * 256, src * QH * TOK + (pair + 1) * 256)
                scores = contract(keys, qall[cols], 1, 1) + bias
                new = jnp.max(scores, axis=0, keepdims=True)
                if not first:
                    old = peak[:, cols]
                    new = jnp.maximum(old, new)
                weights = jnp.exp2((scores - new) * SCALE2)
                total = jnp.sum(weights, axis=0, keepdims=True)
                summed = contract(values, weights.astype(BF16), 0, 0)
                if not first:
                    fade = jnp.exp2((old - new) * SCALE2)
                    total += den[:, cols] * fade
                    summed += acc[:, cols] * fade
                peak[:, cols] = new
                den[:, cols] = total
                acc[:, cols] = summed

    def attend_step(s):
        if s < half:
            attend([around(z - s), around(z + s)])
        else:
            attend([around(z - s)])

    hops = iter(range(1, half + 1))
    parts = iter(range(1, half + 1))

    def hop():
        s = next(hops, None)
        if s is not None:
            ring_hop(s)

    def work():
        s = next(parts, None)
        if s is not None:
            attend_step(s)

    hop()
    give_c.wait_recv()
    block_lhs(0)
    block_lhs(1)
    give_q.wait_recv()
    hop()
    attend([z], first=True)
    work()

    for o in range(1, nz):
        k = around(z + o)
        copy(dpair.at[0], adec.at[k], ad_ss.at[o], ad_rs.at[k], at_z(k)).wait_recv()
        copy(pbuf.at[k], arecv.at[k], a_ss.at[o], a_rs.at[k], at_z(k)).wait_recv()
    state = jnp.zeros((rows, 128), F32)
    for k in range(nz):
        pref[k] = state.astype(BF16)
        state = adec[k] * state + arecv[k].astype(F32)
    for o in far_first:
        k = around(z + o)
        start(copy(pref.at[k], sin.at[z], r_ss.at[o], r_rs.at[z], at_z(k)))
    sin[z] = pref[z]

    hop()
    work()
    hop()
    work()
    give_gate.wait_recv()

    for o in range(1, nz):
        k = around(z + o)
        copy(pref.at[k], sin.at[k], r_ss.at[o], r_rs.at[k], at_z(k)).wait_recv()
    squares = [jnp.zeros((TOK, 128), F32) for _ in range(2)]
    for c in range(OWN):
        cols = slice(c * 128, (c + 1) * 128)
        enter = jnp.concatenate([sin[c * per_tile + r] for r in range(per_tile)], axis=0)
        rhs[0, c, TOK:] = enter
        rhs[1, c, TOK:] = (drow[0, c] * enter.astype(F32) + cstate[0, c]).astype(BF16)
        at = y * (2 * OWN) + 2 * c
        skip = jnp.where(lane1 < HEADP, skip_ref[0, at], skip_ref[0, at + 1])
        for t in range(2):
            out = ecum[t, c] * contract(lhs[t], rhs[t, c], 1, 0)
            out += skip * xs[t, :, cols].astype(F32)
            gate = gates[t, :, cols].astype(F32)
            value = out * (gate / (1.0 + jnp.exp(-gate)))
            squares[t] += value * value
            ubuf[t, c] = (value * gain_ref[:, cols]).astype(BF16)
            i = t * OWN + c
            start(copy(ubuf.at[t, c], hrecv.at[y, c], h_ss.at[i], h_rs.at[y, c], in_section(1, t)))
    ones = jnp.ones((8, 128), F32)
    for t in range(2):
        sqsend[t] = contract(ones, squares[t], 1, 1, HIGH)
        i = 2 * OWN + t
        start(copy(sqsend.at[t], sqrecv.at[y], h_ss.at[i], h_rs.at[y, OWN], in_section(1, t)))

    for _ in range(half):
        hop()
        work()

    mine_cols = slice(0, QH * TOK)
    other_cols = slice(QH * TOK, 2 * QH * TOK)
    osend[...] = (acc[:, other_cols] / den[:, other_cols]).astype(BF16)
    stsend[0] = peak[:, other_cols]
    stsend[1] = den[:, other_cols]
    swap = copy(osend, orecv, y_ss.at[7], y_rs.at[7], partner)
    swap_stats = copy(stsend, strecv, y_ss.at[8], y_rs.at[8], partner)
    start(swap_stats)
    start(swap)

    for u in range(2):
        for c in range(OWN):
            copy(ubuf.at[0, c], hrecv.at[u, c], h_ss.at[c], h_rs.at[u, c], partner).wait_recv()
        copy(sqsend.at[0], sqrecv.at[u], h_ss.at[2 * OWN], h_rs.at[u, OWN], partner).wait_recv()
    factor = lax.rsqrt((sqrecv[0] + sqrecv[1]) * (1.0 / FEAT) + 1e-5)
    pick = jnp.where(row[:8] == 0, 1.0, 0.0).astype(F32)
    factor = contract(factor, pick, 0, 0, HIGH)
    for u in range(2):
        for c in range(OWN):
            j = u * OWN + c
            hand_ref[:, j * 128 : (j + 1) * 128] = (hrecv[u, c].astype(F32) * factor).astype(BF16)

    swap_stats.wait_recv()
    swap.wait_recv()
    m1 = peak[:, mine_cols]
    m2 = strecv[0]
    top = jnp.maximum(m1, m2)
    w1 = jnp.exp2((m1 - top) * SCALE2)
    w2 = jnp.exp2((m2 - top) * SCALE2) * strecv[1]
    inv = 1.0 / (w1 * den[:, mine_cols] + w2)
    w1 = w1 * inv
    w2 = w2 * inv
    for h in range(QH):
        cols = slice(h * TOK, (h + 1) * TOK)
        both = acc[:, cols] * w1[:, cols] + orecv[:, cols].astype(F32) * w2[:, cols]
        att_ref[:, cols] = both.T.astype(BF16)

    for c in sent:
        c.wait_send()


def shards(nz, nsec, *args):
    flat = [a.reshape(a.shape[1:]) if a.ndim == 3 else a for a in args]
    rows = OWN * TOK // nz
    half = nz // 2
    order_len = args[-1].shape[1]
    vmem = pl.BlockSpec(memory_space=pltpu.VMEM)
    hbm = pl.BlockSpec(memory_space=pl.ANY)
    dma = pltpu.SemaphoreType.DMA
    handed, attended = pl.pallas_call(
        functools.partial(kernel, nz, nsec),
        out_shape=(
            jax.ShapeDtypeStruct((TOK, FEAT), BF16),
            jax.ShapeDtypeStruct((TOK, QH * 128), BF16),
        ),
        in_specs=[hbm] * 12,
        out_specs=(vmem, vmem),
        scratch_shapes=[
            pltpu.VMEM((2, TOK, OWN * 128), BF16),
            pltpu.VMEM((2, TOK, OWN * 128), BF16),
            pltpu.VMEM((2, TOK, 128), BF16),
            pltpu.VMEM((2, TOK, 128), BF16),
            pltpu.VMEM((2, HEADS, TOK), F32),
            pltpu.SMEM((1, HEADS), F32),
            pltpu.SMEM((1, HEADS), F32),
            pltpu.VMEM((1, OWN * 128), F32),
            pltpu.SMEM((1, order_len), jnp.int32),
            pltpu.VMEM((nz, 2, TOK, 128), BF16),
            pltpu.VMEM((2 * QH * TOK, 128), BF16),
            pltpu.VMEM((1, 2 * QH * TOK), F32),
            pltpu.VMEM((1, 2 * QH * TOK), F32),
            pltpu.VMEM((128, 2 * QH * TOK), F32),
            pltpu.VMEM((2, OWN, TOK, 128), F32),
            pltpu.VMEM((2, OWN, TOK + 128, 128), BF16),
            pltpu.VMEM((2, TOK, TOK + 128), BF16),
            pltpu.VMEM((2, OWN, 1, 128), F32),
            pltpu.VMEM((2, OWN, 128, 128), F32),
            pltpu.VMEM((OWN, 1, 128), F32),
            pltpu.VMEM((nz, rows, 128), BF16),
            pltpu.VMEM((nz, rows, 128), BF16),
            pltpu.VMEM((nz, 1, 128), F32),
            pltpu.VMEM((nz, rows, 128), BF16),
            pltpu.VMEM((nz, rows, 128), BF16),
            pltpu.VMEM((2, OWN, TOK, 128), BF16),
            pltpu.VMEM((2, OWN, TOK, 128), BF16),
            pltpu.VMEM((2, 8, 128), F32),
            pltpu.VMEM((2, 8, 128), F32),
            pltpu.VMEM((128, QH * TOK), BF16),
            pltpu.VMEM((128, QH * TOK), BF16),
            pltpu.VMEM((2, 1, QH * TOK), F32),
            pltpu.VMEM((2, 1, QH * TOK), F32),
            dma((2, half + 1, 2)),
            dma((2, half + 1, 2)),
            dma((9,)),
            dma((9,)),
            dma((nz,)),
            dma((nz,)),
            dma((nz,)),
            dma((nz,)),
            dma((nz,)),
            dma((nz,)),
            dma((2 * OWN + 2,)),
            dma((2, OWN + 1)),
            dma((15,)),
        ],
        compiler_params=pltpu.CompilerParams(
            collective_id=0, has_side_effects=True, vmem_limit_bytes=60 * 1024 * 1024
        ),
        cost_estimate=pl.CostEstimate(
            flops=1300000000, bytes_accessed=1400000, transcendentals=2500000
        ),
    )(*flat)
    return handed[None], attended[None]


def solution(mesh):
    nz = mesh.shape["ctx"] // 2
    nsec = mesh.shape["section"]
    wide = P("section", "ctx", "tp")
    return jax.shard_map(
        functools.partial(shards, nz, nsec),
        mesh=mesh,
        in_specs=(
            wide,
            wide,
            wide,
            wide,
            P("section", "tp", "ctx"),
            P("section", "tp"),
            P("section", "tp"),
            P("section", "tp"),
            wide,
            wide,
            wide,
            P("section", None),
        ),
        out_specs=(wide, wide),
        check_vma=False,
    )
```

time: 80.7 us -> 70 us (0.87)
  local copies, waits for them, and re-layouts: 7.87 us -> 2.36 us
  Pallas kernels: 71.6 us -> 66.3 us
    unnamed x26 -> x4, local copies, waits for them, and re-layouts: 7.87 us -> 2.36 us
    pallas_call x1, Pallas kernels: 71.6 us -> 66.3 us  [shards(): pl.pallas_call(functools.partial(kernel, nz, nsec), out_shape=(jax.ShapeD...]
where the time goes in v2:
time: 70 us; the launch traced here: 69.3 us
  Pallas kernels  66.3 us (95%)
  local copies, waits for them, and re-layouts  2.36 us (3%)
    pallas_call x1, Pallas kernels, shards(): pl.pallas_call(functools.partial(kernel, nz, nsec), out_shape=(jax.ShapeD...  66.3 us
    unnamed x4, local copies, waits for them, and re-layouts  2.36 us

profile of v2, /device:TPU:6, one launch (start us, length us, event | category | flops | bytes accessed | tf_op | source)
XLA Modules:
  0.0 69.3 jit_solution(12196293622527242661)
XLA Ops:
  0.6 66.3 %shard_map.131 = (bf16[128,1024]{1,0:T(8,128)(2,1)}, bf16[128,512]{1,0:T(8,128)(2,1)}) custom-call(bf16[128,1024]{1,0:T(8,128)(2,1)} %bitcast.12, bf16[128,1024]{1,0:T(8,128)(2,1)} %bitcast.13, bf16[128,128]{1,0:T(8,128)(2,1)} %bitcast.15, bf16[128,128]{1,0:T(8,128)(2,1)} %bitcast.16, f32[16,128]{1,0:T(8,128)} %bitcast.19, f32[1,16]{1,0:T(1,128)} %rate_in.1, ...), custom_call_target="tpu_custom_call" | custom-call | flops 1300000000 | bytes 1400000 | tf_op jit(solution)/shard_map/pallas_call | solution.py:436
  66.9 0.0 copy-start
  66.9 1.7 %copy.16 = bf16[1,128,1024]{2,1,0:T(8,128)(2,1)} copy(bf16[1,128,1024]{2,1,0:T(8,128)(2,1)} %bitcast.10) | data formatting | bytes 524288
  68.6 0.0 copy-done
  68.6 0.7 copy.17
Async XLA Ops:
  66.9 1.7 %copy-start = (bf16[128,512]{1,0:T(8,128)(2,1)S(1)}, bf16[128,512]{1,0:T(8,128)(2,1)}, u32[]{:S(2)}) copy-start(bf16[128,512]{1,0:T(8,128)(2,1)} %get-tuple-element.5) | copy-start | bytes 393220

commit v3 on v2

--- a/solution.py
+++ b/solution.py
@@ -21,6 +21,8 @@
 TILES = FEAT // 128
 OWN = TILES // 2
 QH = 4
+SCHEDULE = ("h", "h", "lohwh", "whwhw", "")
+PIECES = 2
 SCALE2 = math.log2(math.e) / math.sqrt(128.0)
 
 
@@ -134,8 +136,8 @@
         (rate_in, rate_ref),
         (x_in.at[:, mine], xs.at[y]),
         (b_in, writes.at[y]),
-        (k_in, kv.at[z, 0]),
-        (v_in, kv.at[z, 1]),
+        (k_in, kv.at[z, 0:TOK]),
+        (v_in, kv.at[z, TOK:]),
         (c_in, reads.at[y]),
         (q_in.at[:, 0:128], qall.at[0:TOK]),
         (q_in.at[:, 128:256], qall.at[TOK : 2 * TOK]),
@@ -184,18 +186,20 @@
     for c in (give_steps, give_b, *give_x):
         start(c)
 
+    piece = 2 * TOK // PIECES
+
     def ring_copy(way, s, t, arriving):
         if way == 0:
             slot, to = around(z - s + (0 if arriving else 1)), around(z + 1)
         else:
             slot, to = around(z + s - (0 if arriving else 1)), around(z - 1)
-        place = kv.at[slot, t]
+        place = kv.at[slot, pl.ds(t * piece, piece)]
         return copy(place, place, kv_ss.at[way, s, t], kv_rs.at[way, s, t], at_z(to))
 
     def ring_parts(s):
         if s < half:
-            return [(w, t) for t in (0, 1) for w in (0, 1)]
-        return [(0, 0), (1, 1)]
+            return [(w, t) for t in range(PIECES) for w in (0, 1)]
+        return [(w, w * PIECES // 2 + t) for t in range(PIECES // 2) for w in (0, 1)]
 
     def ring_hop(s):
         going = ring_parts(s + 1) if s < half else []
@@ -203,6 +207,23 @@
             ring_copy(w, s, t, True).wait_recv()
             if (w, t) in going:
                 start(ring_copy(w, s + 1, t, False))
+
+    hops = iter(range(1, half + 1))
+    parts = iter(range(1, half + 1))
+
+    def run(what):
+        for item in what:
+            if item == "o":
+                give_q.wait_recv()
+                attend([z], first=True)
+            elif item == "l":
+                give_c.wait_recv()
+                block_lhs(0)
+                block_lhs(1)
+            else:
+                s = next(hops if item == "h" else parts, None)
+                if s is not None:
+                    (ring_hop if item == "h" else attend_step)(s)
 
     for f in fetches[:6]:
         f.wait()
@@ -217,18 +238,21 @@
     upper = jnp.where(row <= lane, 1.0, 0.0).astype(F32)
     lane_head = lax.shift_right_logical(lane[:HEADS], 6)
 
+    def spread_of(c):
+        return jnp.where(row16 - y * (2 * OWN) - 2 * c == lane_head, 1.0, 0.0).astype(F32)
+
     def scales_of(t):
         step = steps[t]
         cum = contract(-rate * step, upper, 1, 0, HIGH)
         return jnp.concatenate([jnp.exp(cum), jnp.exp(-cum) * step], axis=1)
 
-    def block_tile(t, scales, c):
+    def block_tile(t, scales, c, t_is_mine):
         cols = slice(c * 128, (c + 1) * 128)
-        spread = jnp.where(row16 - y * (2 * OWN) - 2 * c == lane_head, 1.0, 0.0).astype(F32)
-        spread_out = contract(scales, spread, 0, 0, HIGH)
+        spread_out = contract(scales, spread_of(c), 0, 0, HIGH)
         ecum[t, c] = spread_out[:TOK]
         d = spread_out[TOK - 1 : TOK]
-        drow[t, c] = d
+        if t_is_mine:
+            drow[t, c] = d
         xf = (xs[t, :, cols].astype(F32) * spread_out[TOK:]).astype(BF16)
         rhs[t, c, 0:TOK] = xf
         cstate[t, c] = contract(writes[t], xf, 0, 0) * d
@@ -240,31 +264,37 @@
 
     scales = scales_of(y)
     for c in range(OWN):
-        block_tile(y, scales, c)
+        block_tile(y, scales, c, True)
+    far_first = sorted(range(1, nz), key=lambda o: -min(o, nz - o))
     for f in fetches[6:]:
         f.wait()
+    run(SCHEDULE[0])
+    give_steps.wait_recv()
+    scales = scales_of(1 - y)
+    for c in range(OWN):
+        d = contract(scales[:, TOK - 8 : TOK], spread_of(c), 0, 0, HIGH)[7:8]
+        drow[1 - y, c] = d
+        dpair[c] = drow[y, c] * d
+    for o in far_first:
+        k = around(z + o)
+        start(copy(dpair.at[k // per_tile], adec.at[z], ad_ss.at[o], ad_rs.at[z], at_z(k)))
+    adec[z] = dpair[z // per_tile]
     start(give_c)
     start(give_q)
     start(give_gate)
-    give_steps.wait_recv()
+    run(SCHEDULE[1])
     give_b.wait_recv()
-    scales = scales_of(1 - y)
     for c in range(OWN):
         if c % (OWN // 2) == 0:
             give_x[c // (OWN // 2)].wait_recv()
-        block_tile(1 - y, scales, c)
-        d1 = drow[1, c]
-        dpair[c] = drow[0, c] * d1
-        total = cstate[0, c] * d1 + cstate[1, c]
+        block_tile(1 - y, scales, c, False)
+        total = cstate[0, c] * drow[1, c] + cstate[1, c]
         for r in range(per_tile):
             pbuf[c * per_tile + r] = total[r * rows : (r + 1) * rows].astype(BF16)
-    far_first = sorted(range(1, nz), key=lambda o: -min(o, nz - o))
     for o in far_first:
         k = around(z + o)
-        start(copy(dpair.at[k // per_tile], adec.at[z], ad_ss.at[o], ad_rs.at[z], at_z(k)))
         start(copy(pbuf.at[k], arecv.at[z], a_ss.at[o], a_rs.at[z], at_z(k)))
     arecv[z] = pbuf[z]
-    adec[z] = dpair[z // per_tile]
 
     row_in = jnp.bitwise_and(row, HALF - 1)
     lane1 = lax.broadcasted_iota(jnp.int32, (1, 128), 1)
@@ -276,7 +306,7 @@
 
     qpos = [query_pos(ctx), query_pos(z * 2 + 1 - y)]
 
-    def attend(slots, first=False):
+    def attend(slots, first=False, after_partner=None):
         biases = []
         for slot in slots:
             at = slot * 2 + y
@@ -284,9 +314,9 @@
             o1 = order_ref[0, 2 * at + 1]
             kpos = jnp.where(row < HALF, o0, o1) * HALF + row_in
             biases.append([jnp.where(kpos <= p, 0.0, NEG).astype(F32) for p in qpos])
-        keys = jnp.concatenate([kv[s, 0] for s in slots], axis=0)
-        values = jnp.concatenate([kv[s, 1] for s in slots], axis=0)
-        for src in range(2):
+        keys = jnp.concatenate([kv[s, 0:TOK] for s in slots], axis=0)
+        values = jnp.concatenate([kv[s, TOK:] for s in slots], axis=0)
+        for src in (1, 0):
             bias = jnp.concatenate([b[src] for b in biases], axis=0)
             bias = jnp.concatenate([bias, bias], axis=1)
             for pair in range(QH // 2):
@@ -306,34 +336,33 @@
                 peak[:, cols] = new
                 den[:, cols] = total
                 acc[:, cols] = summed
+            if src == 1 and after_partner is not None:
+                after_partner()
+
+    def partial_copies():
+        return [copy(stsend, strecv, y_ss.at[7], y_rs.at[7], partner)] + [
+            copy(osend.at[h], orecv.at[h], y_ss.at[8 + h], y_rs.at[8 + h], partner)
+            for h in range(QH)
+        ]
+
+    def give_partial():
+        copies = partial_copies()
+        other_cols = slice(QH * TOK, 2 * QH * TOK)
+        stsend[0] = peak[:, other_cols]
+        stsend[1] = den[:, other_cols]
+        start(copies[0])
+        for h in range(QH):
+            cols = slice((QH + h) * TOK, (QH + h + 1) * TOK)
+            osend[h] = (acc[:, cols] / den[:, cols]).astype(BF16)
+            start(copies[1 + h])
 
     def attend_step(s):
         if s < half:
             attend([around(z - s), around(z + s)])
         else:
-            attend([around(z - s)])
-
-    hops = iter(range(1, half + 1))
-    parts = iter(range(1, half + 1))
-
-    def hop():
-        s = next(hops, None)
-        if s is not None:
-            ring_hop(s)
-
-    def work():
-        s = next(parts, None)
-        if s is not None:
-            attend_step(s)
-
-    hop()
-    give_c.wait_recv()
-    block_lhs(0)
-    block_lhs(1)
-    give_q.wait_recv()
-    hop()
-    attend([z], first=True)
-    work()
+            attend([around(z - s)], after_partner=give_partial)
+
+    run(SCHEDULE[2])
 
     for o in range(1, nz):
         k = around(z + o)
@@ -348,10 +377,7 @@
         start(copy(pref.at[k], sin.at[z], r_ss.at[o], r_rs.at[z], at_z(k)))
     sin[z] = pref[z]
 
-    hop()
-    work()
-    hop()
-    work()
+    run(SCHEDULE[3])
     give_gate.wait_recv()
 
     for o in range(1, nz):
@@ -380,19 +406,7 @@
         i = 2 * OWN + t
         start(copy(sqsend.at[t], sqrecv.at[y], h_ss.at[i], h_rs.at[y, OWN], in_section(1, t)))
 
-    for _ in range(half):
-        hop()
-        work()
-
-    mine_cols = slice(0, QH * TOK)
-    other_cols = slice(QH * TOK, 2 * QH * TOK)
-    osend[...] = (acc[:, other_cols] / den[:, other_cols]).astype(BF16)
-    stsend[0] = peak[:, other_cols]
-    stsend[1] = den[:, other_cols]
-    swap = copy(osend, orecv, y_ss.at[7], y_rs.at[7], partner)
-    swap_stats = copy(stsend, strecv, y_ss.at[8], y_rs.at[8], partner)
-    start(swap_stats)
-    start(swap)
+    run(SCHEDULE[4] + "hw" * half)
 
     for u in range(2):
         for c in range(OWN):
@@ -406,8 +420,9 @@
             j = u * OWN + c
             hand_ref[:, j * 128 : (j + 1) * 128] = (hrecv[u, c].astype(F32) * factor).astype(BF16)
 
-    swap_stats.wait_recv()
-    swap.wait_recv()
+    swaps = partial_copies()
+    swaps[0].wait_recv()
+    mine_cols = slice(0, QH * TOK)
     m1 = peak[:, mine_cols]
     m2 = strecv[0]
     top = jnp.maximum(m1, m2)
@@ -418,11 +433,24 @@
     w2 = w2 * inv
     for h in range(QH):
         cols = slice(h * TOK, (h + 1) * TOK)
-        both = acc[:, cols] * w1[:, cols] + orecv[:, cols].astype(F32) * w2[:, cols]
+        swaps[1 + h].wait_recv()
+        both = acc[:, cols] * w1[:, cols] + orecv[h].astype(F32) * w2[:, cols]
         att_ref[:, cols] = both.T.astype(BF16)
 
     for c in sent:
         c.wait_send()
+
+
+def deliver(half_rows, hand_in, att_in, hand_out, att_out, sems):
+    copies = []
+    for i, (src, dst) in enumerate(((hand_in, hand_out), (att_in, att_out))):
+        for p in range(2):
+            part = pl.ds(p * half_rows, half_rows)
+            copies.append(pltpu.make_async_copy(src.at[part], dst.at[part], sems.at[2 * i + p]))
+    for c in copies:
+        c.start()
+    for c in copies:
+        c.wait()
 
 
 def shards(nz, nsec, *args):
@@ -451,7 +479,7 @@
             pltpu.SMEM((1, HEADS), F32),
             pltpu.VMEM((1, OWN * 128), F32),
             pltpu.SMEM((1, order_len), jnp.int32),
-            pltpu.VMEM((nz, 2, TOK, 128), BF16),
+            pltpu.VMEM((nz, 2 * TOK, 128), BF16),
             pltpu.VMEM((2 * QH * TOK, 128), BF16),
             pltpu.VMEM((1, 2 * QH * TOK), F32),
             pltpu.VMEM((1, 2 * QH * TOK), F32),
@@ -471,14 +499,14 @@
             pltpu.VMEM((2, OWN, TOK, 128), BF16),
             pltpu.VMEM((2, 8, 128), F32),
             pltpu.VMEM((2, 8, 128), F32),
-            pltpu.VMEM((128, QH * TOK), BF16),
-            pltpu.VMEM((128, QH * TOK), BF16),
+            pltpu.VMEM((QH, 128, TOK), BF16),
+            pltpu.VMEM((QH, 128, TOK), BF16),
             pltpu.VMEM((2, 1, QH * TOK), F32),
             pltpu.VMEM((2, 1, QH * TOK), F32),
-            dma((2, half + 1, 2)),
-            dma((2, half + 1, 2)),
-            dma((9,)),
-            dma((9,)),
+            dma((2, half + 1, PIECES)),
+            dma((2, half + 1, PIECES)),
+            dma((8 + QH,)),
+            dma((8 + QH,)),
             dma((nz,)),
             dma((nz,)),
             dma((nz,)),
@@ -496,6 +524,17 @@
             flops=1300000000, bytes_accessed=1400000, transcendentals=2500000
         ),
     )(*flat)
+    half_rows = TOK // 2
+    handed, attended = pl.pallas_call(
+        functools.partial(deliver, half_rows),
+        out_shape=(
+            jax.ShapeDtypeStruct((TOK, FEAT), BF16),
+            jax.ShapeDtypeStruct((TOK, QH * 128), BF16),
+        ),
+        in_specs=[hbm, hbm],
+        out_specs=(hbm, hbm),
+        scratch_shapes=[dma((4,))],
+    )(handed, attended)
     return handed[None], attended[None]
 
 

time: 70 us -> 79.7 us (1.14)
  Pallas kernels: 66.3 us -> 79 us
  local copies, waits for them, and re-layouts: 2.36 us -> 0 us
    pallas_call x0 -> x1, Pallas kernels: none -> 13.1 us  [shards(): pl.pallas_call(functools.partial(deliver, half_rows), out_shape=(jax.Shap...]
    unnamed x4 -> x0, local copies, waits for them, and re-layouts: 2.36 us -> none
where the time goes in v3:
time: 79.7 us; the launch traced here: 79.6 us
  Pallas kernels  79 us (99%)
    pallas_call x1, Pallas kernels, shards(): pl.pallas_call(functools.partial(kernel, nz, nsec), out_shape=(jax.ShapeD...  65.9 us
    pallas_call x1, Pallas kernels, shards(): pl.pallas_call(functools.partial(deliver, half_rows), out_shape=(jax.Shap...  13.1 us

profile of v3, /device:TPU:6, one launch (start us, length us, event | category | flops | bytes accessed | tf_op | source)
XLA Modules:
  0.0 79.6 jit_solution(9430637494599001726)
XLA Ops:
  0.6 65.9 %shard_map.131 = (bf16[128,1024]{1,0:T(8,128)(2,1)}, bf16[128,512]{1,0:T(8,128)(2,1)}) custom-call(bf16[128,1024]{1,0:T(8,128)(2,1)} %bitcast.10, bf16[128,1024]{1,0:T(8,128)(2,1)} %bitcast.11, bf16[128,128]{1,0:T(8,128)(2,1)} %bitcast.15, bf16[128,128]{1,0:T(8,128)(2,1)} %bitcast.16, f32[16,128]{1,0:T(8,128)} %bitcast.19, f32[1,16]{1,0:T(1,128)} %rate_in.1, ...), custom_call_target="tpu_custom_call" | custom-call | flops 1300000000 | bytes 1400000 | tf_op jit(solution)/shard_map/pallas_call | solution.py:464
  66.6 13.1 %shard_map.132 = (bf16[128,1024]{1,0:T(8,128)(2,1)}, bf16[128,512]{1,0:T(8,128)(2,1)}) custom-call(bf16[128,1024]{1,0:T(8,128)(2,1)} %get-tuple-element.6.hand_in, bf16[128,512]{1,0:T(8,128)(2,1)} %get-tuple-element.7.att_in), custom_call_target="tpu_custom_call" | custom-call | tf_op jit(solution)/shard_map/pallas_call | solution.py:528

commit v4 on v3

--- a/solution.py
+++ b/solution.py
@@ -239,16 +239,22 @@
     lane_head = lax.shift_right_logical(lane[:HEADS], 6)
 
     def spread_of(c):
-        return jnp.where(row16 - y * (2 * OWN) - 2 * c == lane_head, 1.0, 0.0).astype(F32)
+        one = jnp.where(row16 - y * (2 * OWN) - 2 * c == lane_head, 1.0, 0.0).astype(BF16)
+        return jnp.concatenate([one] * 3, axis=0)
 
     def scales_of(t):
         step = steps[t]
         cum = contract(-rate * step, upper, 1, 0, HIGH)
-        return jnp.concatenate([jnp.exp(cum), jnp.exp(-cum) * step], axis=1)
+        whole = jnp.concatenate([jnp.exp(cum), jnp.exp(-cum) * step], axis=1)
+        high = whole.astype(BF16)
+        rest = whole - high.astype(F32)
+        middle = rest.astype(BF16)
+        low = (rest - middle.astype(F32)).astype(BF16)
+        return jnp.concatenate([high, middle, low], axis=0)
 
     def block_tile(t, scales, c, t_is_mine):
         cols = slice(c * 128, (c + 1) * 128)
-        spread_out = contract(scales, spread_of(c), 0, 0, HIGH)
+        spread_out = contract(scales, spread_of(c), 0, 0)
         ecum[t, c] = spread_out[:TOK]
         d = spread_out[TOK - 1 : TOK]
         if t_is_mine:
@@ -272,7 +278,7 @@
     give_steps.wait_recv()
     scales = scales_of(1 - y)
     for c in range(OWN):
-        d = contract(scales[:, TOK - 8 : TOK], spread_of(c), 0, 0, HIGH)[7:8]
+        d = contract(scales[:, 0:TOK], spread_of(c), 0, 0)[TOK - 1 : TOK]
         drow[1 - y, c] = d
         dpair[c] = drow[y, c] * d
     for o in far_first:
@@ -441,16 +447,9 @@
         c.wait_send()
 
 
-def deliver(half_rows, hand_in, att_in, hand_out, att_out, sems):
-    copies = []
-    for i, (src, dst) in enumerate(((hand_in, hand_out), (att_in, att_out))):
-        for p in range(2):
-            part = pl.ds(p * half_rows, half_rows)
-            copies.append(pltpu.make_async_copy(src.at[part], dst.at[part], sems.at[2 * i + p]))
-    for c in copies:
-        c.start()
-    for c in copies:
-        c.wait()
+def deliver(hand_in, att_in, hand_out, att_out):
+    hand_out[...] = hand_in[...]
+    att_out[...] = att_in[...]
 
 
 def shards(nz, nsec, *args):
@@ -524,16 +523,14 @@
             flops=1300000000, bytes_accessed=1400000, transcendentals=2500000
         ),
     )(*flat)
-    half_rows = TOK // 2
     handed, attended = pl.pallas_call(
-        functools.partial(deliver, half_rows),
+        deliver,
         out_shape=(
             jax.ShapeDtypeStruct((TOK, FEAT), BF16),
             jax.ShapeDtypeStruct((TOK, QH * 128), BF16),
         ),
-        in_specs=[hbm, hbm],
-        out_specs=(hbm, hbm),
-        scratch_shapes=[dma((4,))],
+        in_specs=[vmem, vmem],
+        out_specs=(vmem, vmem),
     )(handed, attended)
     return handed[None], attended[None]
 

time: 79.7 us -> 66.7 us (0.84)
  Pallas kernels: 79 us -> 65.8 us
    pallas_call x1, Pallas kernels: 13.1 us -> 1.74 us  [shards(): pl.pallas_call(deliver, out_shape=(jax.ShapeDtypeStruct((TOK, FEAT), BF16...]
    pallas_call x1, Pallas kernels: 65.9 us -> 64.1 us  [shards(): pl.pallas_call(functools.partial(kernel, nz, nsec), out_shape=(jax.ShapeD...]
where the time goes in v4:
time: 66.7 us; the launch traced here: 66.4 us
  Pallas kernels  65.8 us (99%)
    pallas_call x1, Pallas kernels, shards(): pl.pallas_call(functools.partial(kernel, nz, nsec), out_shape=(jax.ShapeD...  64.1 us
    pallas_call x1, Pallas kernels, shards(): pl.pallas_call(deliver, out_shape=(jax.ShapeDtypeStruct((TOK, FEAT), BF16...  1.74 us

profile of v4, /device:TPU:6, one launch (start us, length us, event | category | flops | bytes accessed | tf_op | source)
XLA Modules:
  0.0 66.4 jit_solution(8678817229275877393)
XLA Ops:
  0.6 64.1 %shard_map.131 = (bf16[128,1024]{1,0:T(8,128)(2,1)}, bf16[128,512]{1,0:T(8,128)(2,1)}) custom-call(bf16[128,1024]{1,0:T(8,128)(2,1)} %bitcast.10, bf16[128,1024]{1,0:T(8,128)(2,1)} %bitcast.11, bf16[128,128]{1,0:T(8,128)(2,1)} %bitcast.15, bf16[128,128]{1,0:T(8,128)(2,1)} %bitcast.16, f32[16,128]{1,0:T(8,128)} %bitcast.19, f32[1,16]{1,0:T(1,128)} %rate_in.1, ...), custom_call_target="tpu_custom_call" | custom-call | flops 1300000000 | bytes 1400000 | tf_op jit(solution)/shard_map/pallas_call | solution.py:463
  64.7 1.7 %shard_map.132 = (bf16[128,1024]{1,0:T(8,128)(2,1)}, bf16[128,512]{1,0:T(8,128)(2,1)}) custom-call(bf16[128,1024]{1,0:T(8,128)(2,1)} %get-tuple-element.6.hand_in, bf16[128,512]{1,0:T(8,128)(2,1)} %get-tuple-element.7.att_in), custom_call_target="tpu_custom_call" | custom-call | tf_op jit(solution)/shard_map/pallas_call | solution.py:526
